TPU v7x, 512 devices: a whole 4x8x8 slice. The times are simulated.
512 devices in a mesh: rep: 32 (over z, y_lo), shard: 16 (over y_hi, x, core).
Axes of the slice: x: 4, y: 8 (y_hi: 2, y_lo: 4; y = y_hi * 4 + y_lo), z: 8, core: 2. Of those that a mesh axis runs over, the one named last changes fastest.
Arguments:
- layer_inputs: bfloat16 [8192, 3072], P('rep', 'shard'), may hold values from -42 to 42
- output_cotangents: bfloat16 [8192, 3072], P('rep', 'shard'), may hold values from -42 to 42
- valid: int32 [8192], P('rep'), may hold values from 0 to 1, as said below
- factor_a_old: float32 [3072, 3072], P('rep', 'shard'), may hold values from -0.6 to 2.5
- factor_g_old: float32 [3072, 3072], P('rep', 'shard'), may hold values from -0.6 to 2.5
- weight_gradient: bfloat16 [3072, 3072], P('shard', 'rep'), may hold values from -0.59765625 to 0.59765625
- basis_g: bfloat16 [3072, 3072], P('shard'), may hold values from -0.109375 to 0.109375
- basis_a: bfloat16 [3072, 3072], P('shard', 'rep'), may hold values from -0.109375 to 0.109375
- spectrum_g: float32 [3072], replicated, may hold values from 0.1 to 1
- spectrum_a: float32 [3072], P('rep'), may hold values from 0.1 to 1
Outputs:
- factor_a_new: float32 [3072, 3072], P('rep', 'shard')
- factor_g_new: float32 [3072, 3072], P('rep', 'shard')
- preconditioned: bfloat16 [3072, 3072], P('shard')
Inputs may be any that keep to these rules, and one draw needn't show every extreme that they name: The first token of every replica has valid = 1.
All inputs are finite; a program needn't handle non-finite values.
Results may differ from a plain program's by a relative error of at most 0.0095.
Values may be sent and summed in bfloat16 or wider, within the bound.
A program may use at most 64 MiB of HBM per device.

v0:
```python
import jax
import jax.numpy as jnp
from jax import lax
from jax.sharding import PartitionSpec as P

DAMPING = 0.03
DECAY = 0.95


def local(
    layer_inputs,
    output_cotangents,
    valid,
    factor_a_old,
    factor_g_old,
    weight_gradient,
    basis_g,
    basis_a,
    spectrum_g,
    spectrum_a,
):
    count = lax.psum(jnp.sum(valid).astype(jnp.float32), "rep")
    weights = valid.astype(jnp.bfloat16)[:, None]
    masked_inputs = layer_inputs * weights
    masked_outputs = output_cotangents * weights
    full_inputs, full_outputs = (
        lax.all_gather(layer_inputs, "shard", axis=1, tiled=True),
        lax.all_gather(output_cotangents, "shard", axis=1, tiled=True),
    )
    local_width = layer_inputs.shape[1]
    term_a = lax.dot_general(
        full_inputs, masked_inputs, (((0,), (0,)), ((), ())), preferred_element_type=jnp.float32
    )
    term_g = lax.dot_general(
        full_outputs, masked_outputs, (((0,), (0,)), ((), ())), preferred_element_type=jnp.float32
    )
    summed = lax.psum_scatter(
        jnp.concatenate([term_a, term_g], axis=1).astype(jnp.bfloat16),
        "rep",
        scatter_dimension=0,
        tiled=True,
    ).astype(jnp.float32)
    scale = (1.0 - DECAY) / count
    factor_a_new = DECAY * factor_a_old + summed[:, :local_width] * scale
    factor_g_new = DECAY * factor_g_old + summed[:, local_width:] * scale
    basis_cols = lax.all_gather(basis_a, "shard", axis=0, tiled=True)
    block = basis_cols
    rotated_in = jnp.dot(
        lax.all_gather(weight_gradient, "rep", axis=1, tiled=True),
        block,
        preferred_element_type=jnp.float32,
    ).astype(jnp.bfloat16)
    rotated_part = lax.dot_general(
        basis_g, rotated_in, (((0,), (0,)), ((), ())), preferred_element_type=jnp.float32
    )
    rotated = lax.psum(rotated_part, "shard")
    scaled = (rotated / (spectrum_g[:, None] * spectrum_a[None, :] + DAMPING)).astype(jnp.bfloat16)
    back_out = jnp.dot(basis_g, scaled, preferred_element_type=jnp.float32).astype(jnp.bfloat16)
    basis_rows = lax.all_to_all(basis_cols, "rep", split_axis=0, concat_axis=1, tiled=True)
    block = basis_rows
    local_block = lax.dot_general(
        lax.all_gather(back_out, "rep", axis=1, tiled=True),
        block,
        (((1,), (1,)), ((), ())),
        preferred_element_type=jnp.float32,
    ).astype(jnp.bfloat16)
    preconditioned = lax.all_gather(local_block, "rep", axis=1, tiled=True)
    return (factor_a_new, factor_g_new, preconditioned)


def solution(mesh):
    placed = (
        P("rep", "shard"),
        P("rep", "shard"),
        P("rep"),
        P("rep", "shard"),
        P("rep", "shard"),
        P("shard", "rep"),
        P("shard", None),
        P("shard", "rep"),
        P(),
        P("rep"),
    )
    return jax.shard_map(
        local,
        mesh=mesh,
        in_specs=placed,
        out_specs=(P("rep", "shard"), P("rep", "shard"), P("shard", None)),
        check_vma=False,
    )
```

profile of v0, /device:TPU:6, one launch (start us, length us, event | category | flops | bytes accessed | tf_op | source)
XLA Modules:
  0.0 982.1 jit_solution(12458968215820440992)
XLA Ops:
  7.2 0.0 copy-start
  7.2 0.0 all-gather.10.cloned.1.call-start
  7.2 1.6 copy.24
  8.8 0.0 all-gather.10.cloned.1.call-update
  8.9 0.0 all-reduce.2.cloned.1.call-start
  8.9 26.3 %all_gather.21 = bf16[3072,96]{1,0:T(8,128)(2,1)S(1)} all-gather(bf16[192,96]{1,0:T(8,128)(2,1)} %param.17), channel_id=1, replica_groups=mesh['rep'=32,'shard'=16] {'shard'}, dimensions={0}, use_global_device_ids=true | all-gather | bytes 626688 | tf_op jit(solution)/shard_map/all_gather | solution.py:46
  35.2 0.0 copy-start.1
  35.2 0.0 copy-start.9
  35.2 0.0 copy-start.10
  35.2 136.4 %all-gather.10.cloned.1.call-done = bf16[192,3072]{0,1:T(8,128)(2,1)} async-done(((bf16[192,96]{0,1:T(8,128)(2,1)}), bf16[192,3072]{0,1:T(8,128)(2,1)}) %all-gather.10.cloned.1.call-update) | async-done | bytes 1179664 | tf_op jit(solution)/shard_map/all_gather | solution.py:49
  171.6 0.0 copy-done
  171.6 3.4 convolution_bitcast_fusion
  175.0 0.0 copy-done.1
  175.0 0.0 all-reduce.2.cloned.1.call-update
  175.0 0.0 all-gather.8.cloned.1.call-start
  175.1 0.7 all-gather.8.cloned.1.call-update
  175.7 0.0 all-gather.6.cloned.1.call-start
  175.8 0.5 all-gather.6.cloned.1.call-update
  176.3 0.0 copy-start.8
  176.3 0.0 copy-start.4
  176.3 0.0 all-gather.12.cloned.1.call-start
  176.4 180.8 %all-reduce.2.cloned.1.call-done = f32[3072,96]{0,1:T(8,128)} async-done(((f32[3072,96]{0,1:T(8,128)}), f32[3072,96]{0,1:T(8,128)}) %all-reduce.2.cloned.1.call-update) | async-done | bytes 1179664 | tf_op jit(solution)/shard_map/psum | solution.py:56
  357.2 0.0 copy-done.9
  357.2 0.0 copy-done.10
  357.2 2.4 fusion.2
  359.6 0.0 copy-start.5
  359.6 0.0 all-gather.12.cloned.1.call-update
  359.7 0.0 reduce-scatter.4.cloned.1.call-start
  359.7 0.0 copy-done.8
  359.7 0.6 fusion.12
  360.3 66.1 %all-gather.8.cloned.1.call-done = bf16[256,3072]{0,1:T(8,128)(2,1)} async-done(((bf16[256,192]{0,1:T(8,128)(2,1)}), bf16[256,3072]{0,1:T(8,128)(2,1)}) %all-gather.8.cloned.1.call-update) | async-done | bytes 1572880 | tf_op jit(solution)/shard_map/all_gather | solution.py:28
  426.4 0.0 copy-done.4
  426.4 3.1 fusion.1
  429.5 60.5 %all-gather.6.cloned.1.call-done = bf16[256,3072]{0,1:T(8,128)(2,1)} async-done(((bf16[256,192]{0,1:T(8,128)(2,1)}), bf16[256,3072]{0,1:T(8,128)(2,1)}) %all-gather.6.cloned.1.call-update) | async-done | bytes 1572880 | tf_op jit(solution)/shard_map/all_gather | solution.py:27
  490.0 0.0 copy-done.5
  490.0 0.0 copy-start.3
  490.0 2.2 fusion
  492.2 0.0 copy-done.3
  492.2 0.2 pad_maximum_fusion
  492.3 2.5 copy.30
  494.8 0.0 copy-start.2
  494.8 0.0 reduce-scatter.4.cloned.1.call-update
  494.8 0.0 all-gather.14.cloned.1.call-start
  494.9 1.1 copy-done.2
  495.9 37.2 %all_to_all.19 = bf16[32,96,96]{2,1,0:T(8,128)(2,1)S(1)} all-to-all(bf16[32,96,96]{2,1,0:T(8,128)(2,1)S(1)} %bitcast.19), channel_id=1, replica_groups=mesh['rep'=32,'shard'=16] {'rep'}, dimensions={0} | all-to-all | bytes 1179648 | tf_op jit(solution)/shard_map/all_to_all | solution.py:59
  533.1 0.3 copy.25
  533.4 0.0 copy-start.6
  533.4 1.1 all_to_all.17
  534.5 0.0 copy-start.7
  534.5 114.9 %all-gather.12.cloned.1.call-done = bf16[192,3072]{0,1:T(8,128)(2,1)} async-done(((bf16[192,96]{0,1:T(8,128)(2,1)}), bf16[192,3072]{0,1:T(8,128)(2,1)}) %all-gather.12.cloned.1.call-update) | async-done | bytes 1179664 | tf_op jit(solution)/shard_map/all_gather | solution.py:62
  649.4 2.1 convolution_convert_fusion.2
  651.5 0.7 copy.26
  652.2 0.0 all-gather.14.cloned.1.call-update
  652.9 79.9 %psum.14 = f32[]{:T(128)} all-reduce(f32[]{:T(128)S(6)} %convert_element_type.27), channel_id=1, replica_groups=mesh['rep'=32,'shard'=16] {'rep'}, use_global_device_ids=true, to_apply=%region_2.0 | all-reduce | flops 1 | bytes 8 | tf_op jit(solution)/shard_map/psum | solution.py:22
  732.8 0.0 copy-done.6
  732.8 0.1 copy.22
  732.9 0.0 copy-done.7
  732.9 0.1 copy.23
  733.7 84.4 %reduce-scatter.4.cloned.1.call-done = bf16[96,384]{1,0:T(8,128)(2,1)} async-done(((bf16[3072,384]{1,0:T(8,128)(2,1)}), bf16[96,384]{1,0:T(8,128)(2,1)}) %reduce-scatter.4.cloned.1.call-update) | async-done | bytes 73744
  818.1 1.0 copy.31
  819.1 0.7 copy.28
  819.9 0.7 copy.27
  820.6 152.2 %all-gather.14.cloned.1.call-done = bf16[192,3072]{0,1:T(8,128)(2,1)} async-done(((bf16[192,96]{0,1:T(8,128)(2,1)}), bf16[192,3072]{0,1:T(8,128)(2,1)}) %all-gather.14.cloned.1.call-update) | async-done | bytes 1179664 | tf_op jit(solution)/shard_map/all_gather | solution.py:67
  972.8 2.5 copy.29
  (2 shorter events, 0.1 us)
Async XLA Ops:
  7.2 164.4 %copy-start = (bf16[192,3072]{1,0:T(8,128)(2,1)S(1)}, bf16[192,3072]{1,0:T(8,128)(2,1)}, u32[]{:S(2)}) copy-start(bf16[192,3072]{1,0:T(8,128)(2,1)} %param.16) | copy-start | bytes 3538948
  7.2 164.4 %all-gather.10.cloned.1.call-start = ((), (), s32[]{:S(2)}) async-start(), calls=%async_computation.4 | async-start | bytes 1622016 | tf_op jit(solution)/shard_map/all_gather | solution.py:49
  8.9 348.3 %all-reduce.2.cloned.1.call-start = ((), (), s32[]{:S(2)}) async-start(), calls=%async_computation.5 | async-start | bytes 2359296 | tf_op jit(solution)/shard_map/psum | solution.py:56
  35.2 139.8 %copy-start.1 = (bf16[3072,96]{1,0:T(8,128)(2,1)}, bf16[3072,96]{1,0:T(8,128)(2,1)S(1)}, u32[]{:S(2)}) copy-start(bf16[3072,96]{1,0:T(8,128)(2,1)S(1)} %all_gather.21) | copy-start | bytes 1769476
  35.2 322.0 %copy-start.9 = (f32[3072]{0:T(1024)S(1)}, f32[3072]{0:T(1024)}, u32[]{:S(2)}) copy-start(f32[3072]{0:T(1024)} %param.18) | copy-start | bytes 36868
  35.2 322.0 %copy-start.10 = (f32[96]{0:T(128)S(1)}, f32[96]{0:T(128)}, u32[]{:S(2)}) copy-start(f32[96]{0:T(128)} %param.19) | copy-start | bytes 1156
  175.0 251.4 %all-gather.8.cloned.1.call-start = ((), (), s32[]{:S(2)}) async-start(), calls=%async_computation.3 | async-start | bytes 1671168 | tf_op jit(solution)/shard_map/all_gather | solution.py:28
  175.7 314.2 %all-gather.6.cloned.1.call-start = ((), (), s32[]{:S(2)}) async-start(), calls=%async_computation.2 | async-start | bytes 1671168 | tf_op jit(solution)/shard_map/all_gather | solution.py:27
  176.3 183.4 %copy-start.8 = (s32[256]{0:T(256)S(1)}, s32[256]{0:T(256)}, u32[]{:S(2)}) copy-start(s32[256]{0:T(256)} %param.12) | copy-start | bytes 3076
  176.3 250.1 %copy-start.4 = (bf16[256,192]{0,1:T(8,128)(2,1)S(1)}, bf16[256,192]{0,1:T(8,128)(2,1)}, u32[]{:S(2)}) copy-start(bf16[256,192]{0,1:T(8,128)(2,1)} %param.11) | copy-start | bytes 294916
  176.3 473.0 %all-gather.12.cloned.1.call-start = ((), (), s32[]{:S(2)}) async-start(), calls=%async_computation.6 | async-start | bytes 1622016 | tf_op jit(solution)/shard_map/all_gather | solution.py:62
  359.6 130.4 %copy-start.5 = (bf16[256,192]{0,1:T(8,128)(2,1)S(1)}, bf16[256,192]{0,1:T(8,128)(2,1)}, u32[]{:S(2)}) copy-start(bf16[256,192]{0,1:T(8,128)(2,1)} %param.10) | copy-start | bytes 294916
  359.7 458.4 %reduce-scatter.4.cloned.1.call-start = ((), (), s32[]{:S(2)}) async-start(), calls=%async_computation.8 | async-start | bytes 2433024
  490.0 2.2 copy-start.3
  494.8 1.1 copy-start.2
  494.8 478.0 %all-gather.14.cloned.1.call-start = ((), (), s32[]{:S(2)}) async-start(), calls=%async_computation.7 | async-start | bytes 1622016 | tf_op jit(solution)/shard_map/all_gather | solution.py:67
  533.4 199.4 %copy-start.6 = (f32[96,192]{1,0:T(8,128)S(1)}, f32[96,192]{1,0:T(8,128)}, u32[]{:S(2)}) copy-start(f32[96,192]{1,0:T(8,128)} %param.13) | copy-start | bytes 221188
  534.5 198.4 %copy-start.7 = (f32[96,192]{1,0:T(8,128)S(1)}, f32[96,192]{1,0:T(8,128)}, u32[]{:S(2)}) copy-start(f32[96,192]{1,0:T(8,128)} %param.14) | copy-start | bytes 221188
Sparse Core Ops, SparseCore 0:
  10.7 160.8 all-gather.9
  175.1 182.0 all-reduce.1
  360.5 65.8 all-gather.7
  429.6 60.3 all-gather.5
  492.5 156.8 all-gather.11
  652.1 165.9 reduce-scatter.3
  820.7 152.0 all-gather.13
where the time goes:
time: 983 us; the launch traced here: 982 us
  waiting for transfers between devices  796 us (81%)
  blocking collectives  143 us (15%)
  between operations  15.6 us (2%)
  matrix products  13.2 us (1%)
  local copies, waits for them, and re-layouts  12.4 us (1%)
    psum x1, waiting for transfers between devices, local(): rotated = lax.psum(rotated_part, 'shard')  181 us
    all_gather x1, waiting for transfers between devices, local(): preconditioned = lax.all_gather(local_block, 'rep', axis=1, tiled=True)  152 us
    all_gather x1, waiting for transfers between devices, local(): lax.all_gather(weight_gradient, 'rep', axis=1, tiled=True)  136 us
    all_gather x1, waiting for transfers between devices, local(): lax.all_gather(back_out, 'rep', axis=1, tiled=True)  115 us
    unnamed x8, waiting for transfers between devices  85.6 us
    psum x1, blocking collectives, local(): count = lax.psum(jnp.sum(valid).astype(jnp.float32), 'rep')  79.9 us
    all_gather x1, waiting for transfers between devices, local(): lax.all_gather(output_cotangents, 'shard', axis=1, tiled=True)  66.1 us
    all_gather x1, waiting for transfers between devices, local(): lax.all_gather(layer_inputs, 'shard', axis=1, tiled=True)  60.5 us
  transfers between devices with their start and end apart: 7, of which 7 were waited for; matrix products, arithmetic and copies ran while one was open for 2% of the time, Pallas kernels for 0%

commit v1 on v0

v1 whole, which is shorter than its diff:
```python
import jax
import jax.numpy as jnp
from jax import lax
from jax.experimental import pallas as pl
from jax.experimental.pallas import tpu as pltpu
from jax.sharding import PartitionSpec as P

DAMPING = 0.03
DECAY = 0.95

NZ, NY, NQ, NX = 8, 4, 8, 4
BF, F32 = jnp.bfloat16, jnp.float32
NT = (((1,), (1,)), ((), ()))
TN = (((0,), (0,)), ((), ()))


def dot(a, b, dims=(((1,), (0,)), ((), ()))):
    return lax.dot_general(a, b, dims, preferred_element_type=F32)


def lanes4(parts):
    return jnp.concatenate([p.astype(F32) for p in parts], axis=1).astype(BF)


def kernel(
    xa, xg, mask, fa_old, fg_old, grad, bg, ba, sg, sa,
    fa_new, fg_new, out,
    d_buf, r_buf, c_buf, bap, az_s, az, cnt_y, cnt_s, cnt_z,
    gy, gfull, bcols, pt, half_s, half_r, keep, rs_s, rs_r, sc,
    boy, pz_s, pz, py,
    gy_ss, gy_rs, ring_ss, ring_rs, b_ss, b_rs, bf_ss, bf_rs,
    r1_ss, r2_ss, r3_ss, r_rs, c_ss, c_rs, n_ss, n_rs, m_ss, m_rs,
    h_ss, h_rs, p_ss, p_rs, s_ss, s_rs, sf_ss, sf_rs,
    a_ss, a_rs, o_ss, o_rs, z_ss, z_rs, q_ss, q_rs,
):
    r = lax.axis_index("rep")
    s = lax.axis_index("shard")
    z, y = lax.div(r, NY), lax.rem(r, NY)
    q, c = lax.div(s, 2), lax.rem(s, 2)
    yh, x = lax.div(q, NX), lax.rem(q, NX)
    half = lax.div(y, 2)

    def y_of(k):
        return lax.rem(y + k, NY)

    def z_of(k):
        return lax.rem(z + k, NZ)

    def q_of(k):
        return lax.rem(q + k, NQ)

    def y_dev(k):
        return (z * NY + y_of(k), s)

    def z_dev(k):
        return (z_of(k) * NY + y, s)

    def q_dev(k):
        return (r, q_of(k) * 2 + c)

    def x_dev(k):
        return (r, (yh * NX + lax.rem(x + k, NX)) * 2 + c)

    sib = (r, q * 2 + 1 - c)

    def far(src, dst, ss, rs, dev):
        return pltpu.make_async_remote_copy(
            src_ref=src, dst_ref=dst, send_sem=ss, recv_sem=rs,
            device_id=dev, device_id_type=pl.DeviceIdType.MESH,
        )

    def each(n, first=1):
        def deco(body):
            def step(k, carry):
                body(k)
                return carry
            lax.fori_loop(first, n, step, 0)
        return deco

    gate = pltpu.get_barrier_semaphore()

    def greet(dev):
        pl.semaphore_signal(gate, inc=1, device_id=dev, device_id_type=pl.DeviceIdType.MESH)

    each(NY)(lambda k: greet(y_dev(k)))
    each(NZ)(lambda k: greet(z_dev(k)))
    each(NQ)(lambda k: greet(q_dev(k)))
    greet(sib)
    own_piece = jnp.logical_and(half == c, yh == c)

    @each(NY, 0)
    def _(j):
        itself = jnp.logical_and(own_piece, j == y)

        @pl.when(jnp.logical_not(itself))
        def _():
            greet((z * NY + j, (c * NX + x) * 2 + half))

    pl.semaphore_wait(gate, 3 + 7 + 7 + 1 + 4 - jnp.where(own_piece, 1, 0))

    @each(NY)
    def _(k):
        far(grad, gy.at[y], gy_ss.at[k], gy_rs.at[k], y_dev(k)).start()

    b_own = bcols.at[pl.ds(pl.multiple_of(s * 192, 64), 192), :]

    @each(NQ)
    def _(k):
        far(ba, b_own, b_ss.at[k], b_rs.at[k], q_dev(k)).start()

    far(ba, b_own, bf_ss.at[0], bf_rs.at[0], sib).start()

    m = mask[...].astype(F32)
    d_buf[:, 0:256] = xa[...]
    d_buf[:, 256:512] = xg[...]
    d_buf[:, 512:640] = jnp.concatenate(
        [ba[...].astype(F32), jnp.zeros((192, 32), F32)], axis=1
    ).astype(BF)

    def piece(h, t):
        dev = (z * NY + 2 * c + h, (t * NX + x) * 2 + yh)
        itself = jnp.logical_and(dev[0] == r, dev[1] == s)
        src = d_buf.at[pl.ds(96 * h, 96), :]
        dst = r_buf.at[y, q]
        return itself, src, dst, far(src, dst, r1_ss.at[2 * h + t], r_rs.at[y, q], dev)

    for h in range(2):
        for t in range(2):
            itself, src, dst, copy = piece(h, t)

            @pl.when(jnp.logical_not(itself))
            def _():
                copy.start()

            @pl.when(itself)
            def _():
                pltpu.make_async_copy(src, dst, r_rs.at[y, q]).start()

    c_own = c_buf.at[y]
    c_own[:, 0:256] = (xa[...].astype(F32) * m).astype(BF)
    c_own[:, 256:512] = (xg[...].astype(F32) * m).astype(BF)
    cnt_y[y] = jnp.broadcast_to(jnp.sum(m, axis=1, keepdims=True), (8, 128))

    @each(NY)
    def _(k):
        far(c_own, c_own, c_ss.at[k], c_rs.at[k], y_dev(k)).start()
        far(cnt_y.at[y], cnt_y.at[y], n_ss.at[k], n_rs.at[k], y_dev(k)).start()

    b_own[...] = ba[...]

    def gather(own, four, full, y_ss, y_rs, ring, between):
        @each(NY)
        def _(k):
            slot = four.at[y_of(NY - k)]
            far(own, slot, y_ss.at[k], y_rs.at[k], y_dev(k)).wait_recv()

        four[y] = own[...]

        def at(zz, rows=pl.ds(0, 192)):
            return full.at[rows, pl.ds(pl.multiple_of(zz * 384, 128), 384)]

        at(z)[...] = lanes4([four[i] for i in range(NY)])
        for k in range(4):
            rows = [pl.ds(0, 192), pl.ds(0, 192)] if k < 3 else [pl.ds(0, 96), pl.ds(96, 96)]
            copies = []
            for way, sign in ((0, NZ - 1), (1, 1)):
                slot = at(z_of(sign * k), rows[way])
                came = at(z_of(sign * (k + 1)), rows[way])
                go = far(slot, slot, ring_ss.at[ring, way, k], ring_rs.at[ring, way, k],
                         z_dev(1 if way == 0 else NZ - 1))
                go.start()
                copies.append((go, far(came, came, ring_ss.at[ring, way, k], ring_rs.at[ring, way, k],
                                       z_dev(1 if way == 0 else NZ - 1))))
            between(k)
            for go, come in copies:
                come.wait_recv()

    def during_first(k):
        slot = r_buf.at[k, c * NX + x]
        far(slot, slot, r2_ss.at[0, k], r_rs.at[k, c * NX + x], x_dev(1)).wait_recv()

        @each(NX)
        def _(j):
            far(slot, slot, r2_ss.at[j, k], r_rs.at[k, c * NX + x], x_dev(j)).start()

        if k == 1:
            @each(NQ)
            def _(j):
                got = bcols.at[pl.ds(pl.multiple_of((q_of(NQ - j) * 2 + c) * 192, 64), 192), :]
                far(got, got, b_ss.at[j], b_rs.at[j], q_dev(j)).wait_recv()
                far(got, got, bf_ss.at[j], bf_rs.at[j], sib).start()

    gather(grad, gy, gfull, gy_ss, gy_rs, 0, during_first)

    @each(NQ, 0)
    def _(j):
        got = bcols.at[pl.ds(pl.multiple_of((q_of(NQ - j) * 2 + 1 - c) * 192, 64), 192), :]
        far(got, got, bf_ss.at[j], bf_rs.at[j], sib).wait_recv()

    rin = dot(gfull[...], bcols[...]).astype(BF)

    def e_block(ref, k, rows=slice(None)):
        return ref.at[rows, pl.ds(pl.multiple_of(q_of(k) * 384, 128), 384)]

    mine = pl.ds(pl.multiple_of(c * 48, 16), 48)
    other = pl.ds(pl.multiple_of((1 - c) * 48, 16), 48)

    @each(NQ, 0)
    def _(k):
        pt[...] = dot(rin, e_block(bg, k)[...], TN)
        keep[k] = pt[mine, :]
        half_s[k] = pt[other, :].astype(BF)
        far(half_s.at[k], half_r.at[k], h_ss.at[k], h_rs.at[k], sib).start()

    @each(NQ)
    def _(k):
        far(half_s.at[k], half_r.at[k], h_ss.at[k], h_rs.at[k], sib).wait_recv()
        rs_s[k] = (keep[k] + half_r[k].astype(F32)).astype(BF)
        far(rs_s.at[k], rs_r.at[k], p_ss.at[k], p_rs.at[k], q_dev(k)).start()

    far(half_s.at[0], half_r.at[0], h_ss.at[0], h_rs.at[0], sib).wait_recv()
    keep[0] = keep[0] + half_r[0].astype(F32)

    @each(NX, 0)
    def _(j):
        col = c * NX + lax.rem(x + NX - j, NX)

        @each(NY, 0)
        def _(k):
            slot = r_buf.at[k, col]

            @pl.when(j > 0)
            def _():
                far(slot, slot, r2_ss.at[j, k], r_rs.at[k, col], x_dev(j)).wait_recv()

            far(slot, slot, r3_ss.at[j, k], r_rs.at[k, col], sib).start()

    @each(NQ)
    def _(k):
        far(rs_s.at[k], rs_r.at[k], p_ss.at[k], p_rs.at[k], q_dev(k)).wait_recv()
        keep[0] = keep[0] + rs_r[k].astype(F32)

    denominator = sa[mine, :] * e_block(sg, 0)[...] + DAMPING
    sc_own = e_block(sc, 0, mine)
    sc_own[...] = (keep[0] / denominator).astype(BF)

    @each(NQ)
    def _(k):
        far(sc_own, sc_own, s_ss.at[k], s_rs.at[k], q_dev(k)).start()

    far(sc_own, sc_own, sf_ss.at[0], sf_rs.at[0], sib).start()

    @each(NX, 0)
    def _(j):
        col = (1 - c) * NX + j

        @each(NY, 0)
        def _(k):
            slot = r_buf.at[k, col]
            far(slot, slot, r3_ss.at[0, 0], r_rs.at[k, col], sib).wait_recv()

    @each(NY)
    def _(k):
        slot = c_buf.at[y_of(NY - k)]
        far(slot, slot, c_ss.at[k], c_rs.at[k], y_dev(k)).wait_recv()
        tile = cnt_y.at[y_of(NY - k)]
        far(tile, tile, n_ss.at[k], n_rs.at[k], y_dev(k)).wait_recv()

    cnt_s[...] = cnt_y[0] + cnt_y[1] + cnt_y[2] + cnt_y[3]

    @each(NZ, 0)
    def _(k):
        to = z_of(k)
        ta = jnp.zeros((96, 192), F32)
        tg = jnp.zeros((96, 192), F32)
        for i in range(NY):
            ta = ta + dot(r_buf[i, to, :, 0:256], c_buf[i, :, 0:256], NT)
            tg = tg + dot(r_buf[i, to, :, 256:512], c_buf[i, :, 256:512], NT)
        az_s[k] = jnp.concatenate([ta, tg], axis=1).astype(BF)
        bap[pl.ds(pl.multiple_of(to * 96, 32), 96), :] = lanes4(
            [r_buf[i, to, :, 512:608] for i in range(NY)]
        )

        @pl.when(k > 0)
        def _():
            far(az_s.at[k], az.at[k], a_ss.at[k], a_rs.at[k], z_dev(k)).start()
            far(cnt_s, cnt_z.at[k], m_ss.at[k], m_rs.at[k], z_dev(k)).start()

    @each(NQ)
    def _(k):
        got = e_block(sc, NQ - k, mine)
        far(got, got, s_ss.at[k], s_rs.at[k], q_dev(k)).wait_recv()
        far(got, got, sf_ss.at[k], sf_rs.at[k], sib).start()

    @each(NQ, 0)
    def _(k):
        got = e_block(sc, NQ - k, other)
        far(got, got, sf_ss.at[k], sf_rs.at[k], sib).wait_recv()

    boy_own = boy.at[y]
    boy_own[...] = dot(bg[...], sc[...], NT).astype(BF)

    @each(NY)
    def _(k):
        far(boy_own, boy_own, o_ss.at[k], o_rs.at[k], y_dev(k)).start()

    @each(NY)
    def _(k):
        slot = boy.at[y_of(NY - k)]
        far(slot, slot, o_ss.at[k], o_rs.at[k], y_dev(k)).wait_recv()

    back = lanes4([boy[i] for i in range(NY)])

    @each(NZ + 1)
    def _(k):
        to = z_of(k)
        part = dot(back, bap[pl.ds(pl.multiple_of(to * 96, 32), 96), :], NT)

        @pl.when(k < NZ)
        def _():
            pz_s[k] = part.astype(BF)
            far(pz_s.at[k], pz.at[k], z_ss.at[k], z_rs.at[k], z_dev(k)).start()

        @pl.when(k == NZ)
        def _():
            pz_s[0] = part.astype(BF)

    total = pz_s[0].astype(F32)
    pt_sum = total
    for k in range(1, NZ):
        far(pz_s.at[k], pz.at[k], z_ss.at[k], z_rs.at[k], z_dev(k)).wait_recv()
        pt_sum = pt_sum + pz[k].astype(F32)
    py_own = py.at[NY]
    py_own[...] = pt_sum.astype(BF)

    @each(NY)
    def _(k):
        far(py_own, py.at[y], q_ss.at[k], q_rs.at[k], y_dev(k)).start()

    def finish_factors(step):
        if step > 0:
            return

        @each(NZ)
        def _(k):
            far(az_s.at[k], az.at[k], a_ss.at[k], a_rs.at[k], z_dev(k)).wait_recv()
            far(cnt_s, cnt_z.at[k], m_ss.at[k], m_rs.at[k], z_dev(k)).wait_recv()

        stat = az_s[0].astype(F32)
        count = cnt_s[...]
        for k in range(1, NZ):
            stat = stat + az[k].astype(F32)
            count = count + cnt_z[k]
        scale = (1.0 - DECAY) / count[0:1, 0:1]
        fa_new[...] = DECAY * fa_old[...] + stat[:, 0:192] * scale
        fg_new[...] = DECAY * fg_old[...] + stat[:, 192:384] * scale

    gather(py_own, py, out, q_ss, q_rs, 1, finish_factors)

    @each(NY)
    def _(k):
        far(grad, gy.at[y], gy_ss.at[k], gy_rs.at[k], y_dev(k)).wait_send()
        far(c_own, c_own, c_ss.at[k], c_rs.at[k], y_dev(k)).wait_send()
        far(cnt_y.at[y], cnt_y.at[y], n_ss.at[k], n_rs.at[k], y_dev(k)).wait_send()
        far(boy_own, boy_own, o_ss.at[k], o_rs.at[k], y_dev(k)).wait_send()
        far(py_own, py.at[y], q_ss.at[k], q_rs.at[k], y_dev(k)).wait_send()

    @each(NQ)
    def _(k):
        far(ba, b_own, b_ss.at[k], b_rs.at[k], q_dev(k)).wait_send()
        far(rs_s.at[k], rs_r.at[k], p_ss.at[k], p_rs.at[k], q_dev(k)).wait_send()
        far(sc_own, sc_own, s_ss.at[k], s_rs.at[k], q_dev(k)).wait_send()
        far(az_s.at[k], az.at[k], a_ss.at[k], a_rs.at[k], z_dev(k)).wait_send()
        far(cnt_s, cnt_z.at[k], m_ss.at[k], m_rs.at[k], z_dev(k)).wait_send()
        far(pz_s.at[k], pz.at[k], z_ss.at[k], z_rs.at[k], z_dev(k)).wait_send()

    @each(NQ, 0)
    def _(k):
        far(ba, b_own, bf_ss.at[k], bf_rs.at[k], sib).wait_send()
        far(half_s.at[k], half_r.at[k], h_ss.at[k], h_rs.at[k], sib).wait_send()
        far(sc_own, sc_own, sf_ss.at[k], sf_rs.at[k], sib).wait_send()

    for h in range(2):
        for t in range(2):
            itself, src, dst, copy = piece(h, t)

            @pl.when(jnp.logical_not(itself))
            def _():
                copy.wait_send()

    @each(NY, 0)
    def _(k):
        slot = r_buf.at[k, q]

        @each(NX)
        def _(j):
            far(slot, slot, r2_ss.at[j, k], r_rs.at[k, q], x_dev(j)).wait_send()

        @each(NX, 0)
        def _(j):
            far(slot, slot, r3_ss.at[j, k], r_rs.at[k, q], sib).wait_send()

    for ring, full in ((0, gfull), (1, out)):
        for k in range(4):
            rows = 192 if k < 3 else 96
            for way in range(2):
                slot = full.at[pl.ds(0, rows), pl.ds(0, 384)]
                far(slot, slot, ring_ss.at[ring, way, k], ring_rs.at[ring, way, k], z_dev(1)).wait_send()


def local(
    layer_inputs,
    output_cotangents,
    valid,
    factor_a_old,
    factor_g_old,
    weight_gradient,
    basis_g,
    basis_a,
    spectrum_g,
    spectrum_a,
):
    V = pltpu.VMEM
    dma = pltpu.SemaphoreType.DMA
    scratch = [
        V((192, 640), BF),
        V((4, 8, 96, 640), BF),
        V((4, 192, 512), BF),
        V((768, 384), BF),
        V((8, 96, 384), BF),
        V((8, 96, 384), BF),
        V((4, 8, 128), F32),
        V((8, 128), F32),
        V((8, 8, 128), F32),
        V((4, 192, 96), BF),
        V((192, 3072), BF),
        V((3072, 96), BF),
        V((96, 384), F32),
        V((8, 48, 384), BF),
        V((8, 48, 384), BF),
        V((8, 48, 384), F32),
        V((8, 48, 384), BF),
        V((8, 48, 384), BF),
        V((96, 3072), BF),
        V((4, 192, 96), BF),
        V((8, 192, 96), BF),
        V((8, 192, 96), BF),
        V((5, 192, 96), BF),
        dma((4,)), dma((4,)),
        dma((2, 2, 4)), dma((2, 2, 4)),
        dma((8,)), dma((8,)), dma((8,)), dma((8,)),
        dma((4,)), dma((4, 4)), dma((4, 4)), dma((4, 8)),
        dma((4,)), dma((4,)), dma((4,)), dma((4,)), dma((8,)), dma((8,)),
        dma((8,)), dma((8,)), dma((8,)), dma((8,)), dma((8,)), dma((8,)), dma((8,)), dma((8,)),
        dma((8,)), dma((8,)), dma((4,)), dma((4,)), dma((8,)), dma((8,)), dma((4,)), dma((4,)),
    ]
    return pl.pallas_call(
        kernel,
        out_shape=(
            jax.ShapeDtypeStruct((96, 192), F32),
            jax.ShapeDtypeStruct((96, 192), F32),
            jax.ShapeDtypeStruct((192, 3072), BF),
        ),
        in_specs=[pl.BlockSpec(memory_space=V)] * 10,
        out_specs=(pl.BlockSpec(memory_space=V),) * 3,
        scratch_shapes=scratch,
        compiler_params=pltpu.CompilerParams(
            collective_id=0, has_side_effects=True, vmem_limit_bytes=48 * 1024 * 1024
        ),
    )(
        layer_inputs.T,
        output_cotangents.T,
        valid[None, :],
        factor_a_old,
        factor_g_old,
        weight_gradient,
        basis_g,
        basis_a,
        spectrum_g[None, :],
        spectrum_a[:, None],
    )


def solution(mesh):
    placed = (
        P("rep", "shard"),
        P("rep", "shard"),
        P("rep"),
        P("rep", "shard"),
        P("rep", "shard"),
        P("shard", "rep"),
        P("shard", None),
        P("shard", "rep"),
        P(),
        P("rep"),
    )
    return jax.shard_map(
        local,
        mesh=mesh,
        in_specs=placed,
        out_specs=(P("rep", "shard"), P("rep", "shard"), P("shard", None)),
        check_vma=False,
    )
```

time: 983 us -> 136 us (0.14)
  waiting for transfers between devices: 796 us -> 0 us
  blocking collectives: 143 us -> 0 us
  Pallas kernels: 0 us -> 124 us
  between operations: 15.6 us -> 0.65 us
  matrix products: 13.2 us -> 0 us
    all_gather x5 -> x0, waiting for transfers between devices: 530 us -> none  [the longest x1 152 us: local(): preconditioned = lax.all_gather(local_block, 'rep', axis=1, tiled=True)]
    psum x1 -> x0, waiting for transfers between devices: 181 us -> none  [local(): rotated = lax.psum(rotated_part, 'shard')]
    pallas_call x0 -> x1, Pallas kernels: none -> 124 us  [local(): pl.pallas_call(kernel, out_shape=(jax.ShapeDtypeStruct((96, 192), F32), j...]
    unnamed x8 -> x0, waiting for transfers between devices: 85.6 us -> none
    psum x1 -> x0, blocking collectives: 79.9 us -> none  [local(): count = lax.psum(jnp.sum(valid).astype(jnp.float32), 'rep')]
    all_to_all x1 -> x0, blocking collectives: 37.2 us -> none  [local(): lax.all_to_all(basis_cols, 'rep', split_axis=0, concat_axis=1, tiled=True)]
    all_gather x1 -> x0, blocking collectives: 26.3 us -> none  [local(): basis_cols = lax.all_gather(basis_a, 'shard', axis=0, tiled=True)]
    dot_general x5 -> x0, matrix products: 13.2 us -> none  [the longest x1 3.38 us: local(): lax.dot_general(basis_g, rotated_in, (((0,), (0,)), ((), ())), preferred_...]
  transfers between devices with their start and end apart: 7 -> 0, of which waited for: 7 -> 0; matrix products, arithmetic and copies ran while one was open for 2% -> 0% of each run, Pallas kernels for 0% -> 0%
where the time goes in v1:
time: 136 us; the launch traced here: 135 us
  Pallas kernels  124 us (91%)
  local copies, waits for them, and re-layouts  10.9 us (8%)
    pallas_call x1, Pallas kernels, local(): pl.pallas_call(kernel, out_shape=(jax.ShapeDtypeStruct((96, 192), F32), j...  124 us
    unnamed x21, local copies, waits for them, and re-layouts  10.1 us

profile of v1, /device:TPU:6, one launch (start us, length us, event | category | flops | bytes accessed | tf_op | source)
XLA Modules:
  0.0 135.3 jit_solution(2418826737288614195)
XLA Ops:
  0.6 0.8 copy.13.sa
  1.4 0.0 copy-start
  1.4 1.3 copy-done
  2.7 0.0 copy-start.1
  2.7 0.9 copy-done.1
  3.5 0.0 copy-start.2
  3.5 0.9 copy-done.2
  4.4 0.0 copy-start.3
  4.4 0.9 copy-done.3
  5.3 0.0 copy-start.4
  5.3 0.9 copy-done.4
  6.2 0.0 copy-start.5
  6.2 0.8 copy-done.5
  7.0 0.0 copy-start.6
  7.0 0.8 copy-done.6
  7.8 0.0 copy-start.7
  7.8 0.7 copy-done.7
  8.5 0.0 copy-start.8
  8.5 0.7 copy-done.8
  9.2 123.8 %shard_map.121 = (f32[96,192]{1,0:T(8,128)S(1)}, f32[96,192]{1,0:T(8,128)S(1)}, bf16[192,3072]{1,0:T(8,128)(2,1)S(1)}) custom-call(bf16[192,256]{1,0:T(8,128)(2,1)S(1)} %bitcast.5, bf16[192,256]{1,0:T(8,128)(2,1)S(1)} %bitcast.6, s32[1,256]{1,0:T(1,128)S(1)} %bitcast.8, f32[96,192]{1,0:T(8,128)S(1)} %copy-done.3, f32[96,192]{1,0:T(8,128)S(1)} %copy-done.4, ...), custom_call_target="tpu_custom_call" | custom-call | tf_op jit(solution)/shard_map/pallas_call | solution.py:457
  133.0 0.6 copy.17
  133.7 0.6 copy.18
  134.3 1.0 copy.19
Async XLA Ops:
  1.4 1.3 copy-start
  2.7 0.9 copy-start.1
  3.5 0.9 copy-start.2
  4.4 0.9 copy-start.3
  5.3 0.9 copy-start.4
  6.2 0.8 copy-start.5
  7.0 0.8 copy-start.6
  7.8 0.7 copy-start.7
  8.5 0.7 copy-start.8

commit v2 on v1

v2 whole, which is shorter than its diff:
```python
import jax
import jax.numpy as jnp
from jax import lax
from jax.experimental import pallas as pl
from jax.experimental.pallas import tpu as pltpu
from jax.sharding import PartitionSpec as P

DAMPING = 0.03
DECAY = 0.95

NZ, NY, NQ, NX = 8, 4, 8, 4
BF, F32 = jnp.bfloat16, jnp.float32
NT = (((1,), (1,)), ((), ()))


def dot(a, b, dims=(((1,), (0,)), ((), ()))):
    return lax.dot_general(a, b, dims, preferred_element_type=F32)


def lanes4(parts):
    return jnp.concatenate([p.astype(F32) for p in parts], axis=1).astype(BF)


def kernel(
    xa_in, xg_in, valid_in, fa_in, fg_in, grad_in, bg_in, ba_in, sg_in, sa_in,
    fa_out, fg_out, out_hbm,
    fa_new, fg_new, out, out_sems,
    xa, xg, valid, fa_old, fg_old, grad, bg, ba, sg, sa, in_sems, sa_col,
    d_buf, r_buf, c_buf, b_buf, r_ba, az_s, az, cnt_y, cnt_s, cnt_z,
    gz, rp_s, rp_r, pt, half_s, half_r, keep, rs_s, rs_r, sc,
    back, boy, pz_s, pz, py,
    gy_ss, gy_rs, g_ss, g_rs, f_ss, f_rs, rb1_ss, rb2_ss, rb3_ss, rb_rs,
    r1_ss, r2_ss, r3_ss, r_rs, c_ss, c_rs, n_ss, n_rs, m_ss, m_rs,
    h_ss, h_rs, p_ss, p_rs, s_ss, s_rs, sf_ss, sf_rs,
    a_ss, a_rs, o_ss, o_rs, z_ss, z_rs, q_ss, q_rs,
):
    r = lax.axis_index("rep")
    s = lax.axis_index("shard")
    z, y = lax.div(r, NY), lax.rem(r, NY)
    q, c = lax.div(s, 2), lax.rem(s, 2)
    yh, x = lax.div(q, NX), lax.rem(q, NX)
    half = lax.div(y, 2)

    def y_of(k):
        return lax.rem(y + k, NY)

    def z_of(k):
        return lax.rem(z + k, NZ)

    def q_of(k):
        return lax.rem(q + k, NQ)

    def y_dev(k):
        return (z * NY + y_of(k), s)

    def z_dev(k):
        return (z_of(k) * NY + y, s)

    def q_dev(k):
        return (r, q_of(k) * 2 + c)

    def x_dev(k):
        return (r, (yh * NX + lax.rem(x + k, NX)) * 2 + c)

    sib = (r, q * 2 + 1 - c)

    def far(src, dst, ss, rs, dev):
        return pltpu.make_async_remote_copy(
            src_ref=src, dst_ref=dst, send_sem=ss, recv_sem=rs,
            device_id=dev, device_id_type=pl.DeviceIdType.MESH,
        )

    def each(n, first=1):
        def deco(body):
            def step(k, carry):
                body(k)
                return carry
            lax.fori_loop(first, n, step, 0)
        return deco

    loads = [
        pltpu.make_async_copy(src, dst, in_sems.at[i])
        for i, (src, dst) in enumerate((
            (grad_in, grad), (ba_in, ba), (xa_in, xa), (xg_in, xg), (valid_in, valid),
            (bg_in, bg), (sg_in, sg), (sa_in, sa), (fa_in, fa_old), (fg_in, fg_old),
        ))
    ]
    for load in loads:
        load.start()

    gate = pltpu.get_barrier_semaphore()

    def greet(dev):
        pl.semaphore_signal(gate, inc=1, device_id=dev, device_id_type=pl.DeviceIdType.MESH)

    each(NY)(lambda k: greet(y_dev(k)))
    each(NZ)(lambda k: greet(z_dev(k)))
    each(NQ)(lambda k: greet(q_dev(k)))
    greet(sib)
    own_piece = jnp.logical_and(half == c, yh == c)

    @each(NY, 0)
    def _(j):
        itself = jnp.logical_and(own_piece, j == y)

        @pl.when(jnp.logical_not(itself))
        def _():
            greet((z * NY + j, (c * NX + x) * 2 + half))

    c_own = c_buf.at[y]
    b_own = b_buf
    for load in loads[:5]:
        load.wait()
    g_own = gz.at[:, pl.ds(pl.multiple_of(z * 128, 128), 128)]
    g_own[:, 0:96] = grad[...]
    g_own[:, 96:128] = jnp.zeros((192, 32), BF)
    b_own[:, 0:96] = ba[...]
    b_own[:, 96:128] = jnp.zeros((192, 32), BF)
    for i in range(NQ):
        r_ba[128 * i + 96 : 128 * i + 128, :] = jnp.zeros((32, 512), BF)
    m = valid[...].reshape(1, 256).astype(F32)
    d_buf[:, 0:256] = xa[...]
    d_buf[:, 256:512] = xg[...]

    pl.semaphore_wait(gate, 3 + 7 + 7 + 1 + 4 - jnp.where(own_piece, 1, 0))

    class Plane:
        def __init__(self, src, slot, ss1, ss2, ss3, rs):
            self.src, self.slot, self.ss1, self.ss2, self.ss3, self.rs = src, slot, ss1, ss2, ss3, rs

        def piece(self, h, t):
            dev = (z * NY + 2 * c + h, (t * NX + x) * 2 + yh)
            itself = jnp.logical_and(dev[0] == r, dev[1] == s)
            src, dst = self.src.at[pl.ds(96 * h, 96), :], self.slot(y, q)
            return itself, src, dst, far(src, dst, self.ss1.at[2 * h + t], self.rs.at[y, q], dev)

        def along_y(self):
            for h in range(2):
                for t in range(2):
                    itself, src, dst, copy = self.piece(h, t)

                    @pl.when(jnp.logical_not(itself))
                    def _():
                        copy.start()

                    @pl.when(itself)
                    def _():
                        pltpu.make_async_copy(src, dst, self.rs.at[y, q]).start()

        def along_x(self, k):
            slot = self.slot(k, c * NX + x)
            far(slot, slot, self.ss2.at[0, k], self.rs.at[k, c * NX + x], x_dev(1)).wait_recv()

            @each(NX)
            def _(j):
                far(slot, slot, self.ss2.at[j, k], self.rs.at[k, c * NX + x], x_dev(j)).start()

            far(slot, slot, self.ss3.at[0, k], self.rs.at[k, c * NX + x], sib).start()

        def to_core(self):
            @each(NX)
            def _(j):
                col = c * NX + lax.rem(x + NX - j, NX)

                @each(NY, 0)
                def _(k):
                    slot = self.slot(k, col)
                    far(slot, slot, self.ss2.at[j, k], self.rs.at[k, col], x_dev(j)).wait_recv()
                    far(slot, slot, self.ss3.at[j, k], self.rs.at[k, col], sib).start()

        def arrive(self):
            @each(NX, 0)
            def _(j):
                col = (1 - c) * NX + j

                @each(NY, 0)
                def _(k):
                    slot = self.slot(k, col)
                    far(slot, slot, self.ss3.at[0, 0], self.rs.at[k, col], sib).wait_recv()

        def sent(self):
            for h in range(2):
                for t in range(2):
                    itself, src, dst, copy = self.piece(h, t)

                    @pl.when(jnp.logical_not(itself))
                    def _():
                        copy.wait_send()

            @each(NY, 0)
            def _(k):
                slot = self.slot(k, q)

                @each(NX)
                def _(j):
                    far(slot, slot, self.ss2.at[j, k], self.rs.at[k, q], x_dev(j)).wait_send()

                @each(NX, 0)
                def _(j):
                    far(slot, slot, self.ss3.at[j, k], self.rs.at[k, q], sib).wait_send()

    def ba_slot(k, col):
        return r_ba.at[pl.ds(pl.multiple_of(col * 128, 128), 96), pl.ds(pl.multiple_of(k * 128, 128), 128)]

    rows_b = Plane(b_own, ba_slot, rb1_ss, rb2_ss, rb3_ss, rb_rs)
    rows_x = Plane(d_buf, lambda k, col: r_buf.at[k, col], r1_ss, r2_ss, r3_ss, r_rs)

    def during_first(k):
        if k == 0:
            rows_b.along_y()
            c_own[:, 0:256] = (xa[...].astype(F32) * m).astype(BF)
            c_own[:, 256:512] = (xg[...].astype(F32) * m).astype(BF)
            cnt_y[y] = jnp.broadcast_to(jnp.sum(m, axis=1, keepdims=True), (8, 128))
        else:
            rows_b.along_x(k - 1)

    @each(NZ)
    def _(k):
        far(g_own, g_own, g_ss.at[k], g_rs.at[k], z_dev(k)).start()

    for k in range(4):
        during_first(k)
    rows_b.along_x(3)
    rows_x.along_y()
    rows_b.to_core()
    rows_b.arrive()

    @each(NZ)
    def _(k):
        got = gz.at[:, pl.ds(pl.multiple_of(z_of(NZ - k) * 128, 128), 128)]
        far(got, got, g_ss.at[k], g_rs.at[k], z_dev(k)).wait_recv()

    def cols_copies(d):
        for way, sign, ok, end in ((0, -1, y >= d, y < NY - 1), (1, 1, y + d < NY, y > 0)):
            slot = c_buf.at[jnp.clip(y + sign * d, 0, NY - 1)]
            who = jnp.clip(y + sign * d, 0, NY - 1)
            to = (jnp.clip(y - sign, 0, NY - 1) + z * NY, s)
            yield ok, jnp.logical_and(ok, end), far(slot, slot, c_ss.at[way, d], c_rs.at[who], to)

    def cols_step(d):
        for ok, onward, copy in cols_copies(d):
            if d > 0:
                pl.when(ok)(copy.wait_recv)
            if d < NY - 1:
                pl.when(onward)(copy.start)

    def y_lanes(ref, i):
        return ref.at[:, pl.ds(pl.multiple_of(i * 128, 128), 128)]

    @each(NY + 1)
    def _(k):
        to = y_of(k)
        y_lanes(rp_s, to)[...] = dot(gz[...], y_lanes(r_ba, to)[...]).astype(BF)

        @pl.when(k < NY)
        def _():
            far(y_lanes(rp_s, to), rp_r.at[k], gy_ss.at[k], gy_rs.at[k], y_dev(k)).start()

    rin = y_lanes(rp_s, y)[...].astype(F32)
    for k in range(1, NY):
        far(y_lanes(rp_s, y), rp_r.at[k], gy_ss.at[k], gy_rs.at[k], y_dev(k)).wait_recv()
        rin = rin + rp_r[k].astype(F32)
    rin = rin.T[0:96, :].astype(BF)

    for load in loads[5:]:
        load.wait()
    sa_row = jnp.concatenate([sa[...].reshape(1, 96), jnp.zeros((1, 32), F32)], axis=1)
    sa_col[...] = jnp.broadcast_to(sa_row, (128, 128)).T[0:96, 0:1]

    def e_block(ref, k, rows=slice(None)):
        return ref.at[rows, pl.ds(pl.multiple_of(q_of(k) * 384, 128), 384)]

    mine = pl.ds(pl.multiple_of(c * 48, 16), 48)
    other = pl.ds(pl.multiple_of((1 - c) * 48, 16), 48)

    @each(NQ, 0)
    def _(k):
        pt[...] = dot(rin, e_block(bg, k)[...])
        keep[k] = pt[mine, :]
        half_s[k] = pt[other, :].astype(BF)
        far(half_s.at[k], half_r.at[k], h_ss.at[k], h_rs.at[k], sib).start()

    @each(NQ)
    def _(k):
        far(half_s.at[k], half_r.at[k], h_ss.at[k], h_rs.at[k], sib).wait_recv()
        rs_s[k] = (keep[k] + half_r[k].astype(F32)).astype(BF)
        far(rs_s.at[k], rs_r.at[k], p_ss.at[k], p_rs.at[k], q_dev(k)).start()

    cols_step(0)

    @each(NY)
    def _(k):
        far(cnt_y.at[y], cnt_y.at[y], n_ss.at[k], n_rs.at[k], y_dev(k)).start()

    far(half_s.at[0], half_r.at[0], h_ss.at[0], h_rs.at[0], sib).wait_recv()
    keep[0] = keep[0] + half_r[0].astype(F32)

    @each(NY, 0)
    def _(k):
        rows_x.along_x(k)

    @each(NQ)
    def _(k):
        far(rs_s.at[k], rs_r.at[k], p_ss.at[k], p_rs.at[k], q_dev(k)).wait_recv()
        keep[0] = keep[0] + rs_r[k].astype(F32)

    sg_here = sg[pl.ds(pl.multiple_of(q * 384, 128), 384)].reshape(1, 384)
    denominator = sa_col[mine, :] * sg_here + DAMPING
    sc_own = e_block(sc, 0, mine)
    sc_own[...] = (keep[0] / denominator).astype(BF)

    @each(NQ)
    def _(k):
        far(sc_own, sc_own, s_ss.at[k], s_rs.at[k], q_dev(k)).start()

    far(sc_own, sc_own, sf_ss.at[0], sf_rs.at[0], sib).start()

    cols_step(1)

    @each(NQ)
    def _(k):
        got = e_block(sc, NQ - k, mine)
        far(got, got, s_ss.at[k], s_rs.at[k], q_dev(k)).wait_recv()
        far(got, got, sf_ss.at[k], sf_rs.at[k], sib).start()

    back[...] = jnp.zeros((192, 96), F32)

    @each(NQ, 0)
    def _(k):
        got = e_block(sc, NQ - k, other)
        far(got, got, sf_ss.at[k], sf_rs.at[k], sib).wait_recv()
        back[...] += dot(e_block(bg, NQ - k)[...], e_block(sc, NQ - k)[...], NT)

    boy_own = y_lanes(boy, y)
    boy_own[:, 0:96] = back[...].astype(BF)
    boy_own[:, 96:128] = jnp.zeros((192, 32), BF)

    @each(NY)
    def _(k):
        far(boy_own, boy_own, o_ss.at[k], o_rs.at[k], y_dev(k)).start()

    cols_step(2)

    @each(NY)
    def _(k):
        slot = y_lanes(boy, y_of(NY - k))
        far(slot, slot, o_ss.at[k], o_rs.at[k], y_dev(k)).wait_recv()

    def pz_half(h, k):
        rows = pl.ds(96 * h, 96)
        return far(pz_s.at[k, rows, :], pz.at[k, rows, :], z_ss.at[h, k], z_rs.at[h, k], z_dev(k))

    @each(NZ + 1)
    def _(k):
        to = z_of(k)
        rows = r_ba[pl.ds(pl.multiple_of(to * 128, 128), 128), :]
        pz_s[k] = dot(boy[...], rows, NT).astype(BF)

        @pl.when(k < NZ)
        def _():
            pz_half(0, k).start()

    each(NZ)(lambda k: pz_half(1, k).start())

    rows_x.to_core()
    rows_x.arrive()

    @each(NY)
    def _(k):
        tile = cnt_y.at[y_of(NY - k)]
        far(tile, tile, n_ss.at[k], n_rs.at[k], y_dev(k)).wait_recv()

    cols_step(3)
    cnt_s[...] = cnt_y[0] + cnt_y[1] + cnt_y[2] + cnt_y[3]

    @each(NZ, 0)
    def _(k):
        to = z_of(k)
        ta = jnp.zeros((96, 192), F32)
        tg = jnp.zeros((96, 192), F32)
        for i in range(NY):
            ta = ta + dot(r_buf[i, to, :, 0:256], c_buf[i, :, 0:256], NT)
            tg = tg + dot(r_buf[i, to, :, 256:512], c_buf[i, :, 256:512], NT)
        az_s[k] = jnp.concatenate([ta, tg], axis=1).astype(BF)

        @pl.when(k > 0)
        def _():
            far(az_s.at[k], az.at[k], a_ss.at[k], a_rs.at[k], z_dev(k)).start()
            far(cnt_s, cnt_z.at[k], m_ss.at[k], m_rs.at[k], z_dev(k)).start()

    def py_half(h, k):
        slot = py.at[y, pl.ds(96 * h, 96), :]
        return far(slot, slot, q_ss.at[h, k], q_rs.at[h, k], y_dev(k))

    for h in range(2):
        rows = slice(96 * h, 96 * h + 96)
        total = pz_s[NZ, rows, :].astype(F32)
        for k in range(1, NZ):
            pz_half(h, k).wait_recv()
            total = total + pz[k, rows, :].astype(F32)
        py[y, rows, :] = total.astype(BF)
        each(NY)(lambda k: py_half(h, k).start())

    def store(i):
        block = pl.ds(pl.multiple_of(z_of(i) * 384, 128), 384)
        return pltpu.make_async_copy(out.at[:, block], out_hbm.at[:, block], out_sems.at[i])

    fa_store = pltpu.make_async_copy(fa_new, fa_out, out_sems.at[8])
    fg_store = pltpu.make_async_copy(fg_new, fg_out, out_sems.at[9])

    def finish_factors(step):
        if step > 0:
            store(step).start()
            store(NZ - step).start()
            return
        store(0).start()

        @each(NZ)
        def _(k):
            far(az_s.at[k], az.at[k], a_ss.at[k], a_rs.at[k], z_dev(k)).wait_recv()
            far(cnt_s, cnt_z.at[k], m_ss.at[k], m_rs.at[k], z_dev(k)).wait_recv()

        stat = az_s[0].astype(F32)
        count = cnt_s[...]
        for k in range(1, NZ):
            stat = stat + az[k].astype(F32)
            count = count + cnt_z[k]
        scale = (1.0 - DECAY) / count[0:1, 0:1]
        fa_new[...] = DECAY * fa_old[...] + stat[:, 0:192] * scale
        fg_new[...] = DECAY * fg_old[...] + stat[:, 192:384] * scale
        fa_store.start()
        fg_store.start()

    def ring_copy(h, way, k, arriving):
        at = z_of((NZ - 1, 1)[way] * (k + arriving))
        lo, n = (96 * h, 96) if k < 3 else (96 * h + 48 * way, 48)
        slot = out.at[pl.ds(lo, n), pl.ds(pl.multiple_of(at * 384, 128), 384)]
        return far(slot, slot, f_ss.at[h, way, k], f_rs.at[h, way, k], z_dev((1, NZ - 1)[way]))

    for k in range(5):
        for h in range(2):
            if k == 0:
                rows = pl.ds(96 * h, 96)
                for j in range(1, NY):
                    py_half(h, j).wait_recv()
                out[rows, pl.ds(pl.multiple_of(z * 384, 128), 384)] = lanes4(
                    [py[i, 96 * h : 96 * h + 96, 0:96] for i in range(NY)]
                )
            for way in range(2):
                if k > 0:
                    ring_copy(h, way, k - 1, 1).wait_recv()
                if k < 4:
                    ring_copy(h, way, k, 0).start()
        if k < 4:
            finish_factors(k)
    store(4).start()

    for i in range(NZ):
        store(i).wait()
    fa_store.wait()
    fg_store.wait()

    @each(NY)
    def _(k):
        far(y_lanes(rp_s, y), rp_r.at[k], gy_ss.at[k], gy_rs.at[k], y_dev(k)).wait_send()
        far(cnt_y.at[y], cnt_y.at[y], n_ss.at[k], n_rs.at[k], y_dev(k)).wait_send()
        far(boy_own, boy_own, o_ss.at[k], o_rs.at[k], y_dev(k)).wait_send()
        py_half(0, k).wait_send()
        py_half(1, k).wait_send()

    @each(NQ)
    def _(k):
        far(rs_s.at[k], rs_r.at[k], p_ss.at[k], p_rs.at[k], q_dev(k)).wait_send()
        far(sc_own, sc_own, s_ss.at[k], s_rs.at[k], q_dev(k)).wait_send()
        far(g_own, g_own, g_ss.at[k], g_rs.at[k], z_dev(k)).wait_send()
        far(az_s.at[k], az.at[k], a_ss.at[k], a_rs.at[k], z_dev(k)).wait_send()
        far(cnt_s, cnt_z.at[k], m_ss.at[k], m_rs.at[k], z_dev(k)).wait_send()
        pz_half(0, k).wait_send()
        pz_half(1, k).wait_send()

    @each(NQ, 0)
    def _(k):
        far(half_s.at[k], half_r.at[k], h_ss.at[k], h_rs.at[k], sib).wait_send()
        far(sc_own, sc_own, sf_ss.at[k], sf_rs.at[k], sib).wait_send()

    for d in range(NY - 1):
        for ok, onward, copy in cols_copies(d):
            pl.when(onward)(copy.wait_send)

    rows_b.sent()
    rows_x.sent()

    for h in range(2):
        for way in range(2):
            for k in range(4):
                ring_copy(h, way, k, 0).wait_send()


def local(
    layer_inputs,
    output_cotangents,
    valid,
    factor_a_old,
    factor_g_old,
    weight_gradient,
    basis_g,
    basis_a,
    spectrum_g,
    spectrum_a,
):
    V = pltpu.VMEM
    dma = pltpu.SemaphoreType.DMA
    scratch = [
        V((96, 192), F32), V((96, 192), F32), V((192, 3072), BF), dma((10,)),
        V((192, 256), BF), V((192, 256), BF), V((256,), jnp.int32),
        V((96, 192), F32), V((96, 192), F32), V((192, 96), BF),
        V((192, 3072), BF), V((192, 96), BF), V((3072,), F32), V((96,), F32), dma((10,)),
        V((96, 1), F32),
        V((192, 512), BF),
        V((4, 8, 96, 512), BF),
        V((4, 192, 512), BF),
        V((192, 128), BF),
        V((1024, 512), BF),
        V((8, 96, 384), BF),
        V((8, 96, 384), BF),
        V((4, 8, 128), F32),
        V((8, 128), F32),
        V((8, 8, 128), F32),
        V((192, 1024), BF),
        V((192, 512), BF),
        V((4, 192, 128), BF),
        V((96, 384), F32),
        V((8, 48, 384), BF),
        V((8, 48, 384), BF),
        V((8, 48, 384), F32),
        V((8, 48, 384), BF),
        V((8, 48, 384), BF),
        V((96, 3072), BF),
        V((192, 96), F32),
        V((192, 512), BF),
        V((9, 192, 128), BF),
        V((8, 192, 128), BF),
        V((4, 192, 128), BF),
        dma((4,)), dma((4,)),
        dma((8,)), dma((8,)), dma((2, 2, 4)), dma((2, 2, 4)),
        dma((4,)), dma((4, 4)), dma((4, 4)), dma((4, 8)),
        dma((4,)), dma((4, 4)), dma((4, 4)), dma((4, 8)),
        dma((2, 4)), dma((4,)), dma((4,)), dma((4,)), dma((8,)), dma((8,)),
        dma((8,)), dma((8,)), dma((8,)), dma((8,)), dma((8,)), dma((8,)), dma((8,)), dma((8,)),
        dma((8,)), dma((8,)), dma((4,)), dma((4,)), dma((2, 8)), dma((2, 8)), dma((2, 4)), dma((2, 4)),
    ]
    return pl.pallas_call(
        kernel,
        out_shape=(
            jax.ShapeDtypeStruct((96, 192), F32),
            jax.ShapeDtypeStruct((96, 192), F32),
            jax.ShapeDtypeStruct((192, 3072), BF),
        ),
        in_specs=[pl.BlockSpec(memory_space=pltpu.HBM)] * 10,
        out_specs=(pl.BlockSpec(memory_space=pltpu.HBM),) * 3,
        scratch_shapes=scratch,
        compiler_params=pltpu.CompilerParams(
            collective_id=0, has_side_effects=True, vmem_limit_bytes=62 * 1024 * 1024
        ),
    )(
        layer_inputs.T,
        output_cotangents.T,
        valid,
        factor_a_old,
        factor_g_old,
        weight_gradient,
        basis_g,
        basis_a,
        spectrum_g,
        spectrum_a,
    )


def solution(mesh):
    placed = (
        P("rep", "shard"),
        P("rep", "shard"),
        P("rep"),
        P("rep", "shard"),
        P("rep", "shard"),
        P("shard", "rep"),
        P("shard", None),
        P("shard", "rep"),
        P(),
        P("rep"),
    )
    return jax.shard_map(
        local,
        mesh=mesh,
        in_specs=placed,
        out_specs=(P("rep", "shard"), P("rep", "shard"), P("shard", None)),
        check_vma=False,
    )
```

time: 136 us -> 118 us (0.87)
  Pallas kernels: 124 us -> 111 us
  local copies, waits for them, and re-layouts: 10.9 us -> 5.44 us
    pallas_call x1, Pallas kernels: 124 us -> 111 us  [local(): pl.pallas_call(kernel, out_shape=(jax.ShapeDtypeStruct((96, 192), F32), j...]
    unnamed x21 -> x3, local copies, waits for them, and re-layouts: 10.1 us -> 5.44 us
where the time goes in v2:
time: 118 us; the launch traced here: 117 us
  Pallas kernels  111 us (94%)
  local copies, waits for them, and re-layouts  5.44 us (5%)
    pallas_call x1, Pallas kernels, local(): pl.pallas_call(kernel, out_shape=(jax.ShapeDtypeStruct((96, 192), F32), j...  111 us
    unnamed x3, local copies, waits for them, and re-layouts  5.44 us

profile of v2, /device:TPU:6, one launch (start us, length us, event | category | flops | bytes accessed | tf_op | source)
XLA Modules:
  0.0 117.1 jit_solution(17733269462772899962)
XLA Ops:
  0.6 111.0 %shard_map.121 = (f32[96,192]{1,0:T(8,128)}, f32[96,192]{1,0:T(8,128)}, bf16[192,3072]{1,0:T(8,128)(2,1)}) custom-call(bf16[192,256]{1,0:T(8,128)(2,1)} %bitcast.2, bf16[192,256]{1,0:T(8,128)(2,1)} %bitcast.3, s32[256]{0:T(256)} %valid_in.1, f32[96,192]{1,0:T(8,128)} %fa_in.1, f32[96,192]{1,0:T(8,128)} %fg_in.1, bf16[192,96]{1,0:T(8,128)(2,1)} %grad_in.1, ...), custom_call_target="tpu_custom_call" | custom-call | tf_op jit(solution)/shard_map/pallas_call | solution.py:552
  111.7 1.5 %copy.16 = f32[96,192]{1,0:T(8,128)} copy(f32[96,192]{1,0:T(8,128)} %get-tuple-element.6) | data formatting | bytes 147456
  113.2 1.5 %copy.17 = f32[96,192]{1,0:T(8,128)} copy(f32[96,192]{1,0:T(8,128)} %get-tuple-element.7) | data formatting | bytes 147456
  114.7 2.4 %copy.18 = bf16[192,3072]{1,0:T(8,128)(2,1)} copy(bf16[192,3072]{1,0:T(8,128)(2,1)} %get-tuple-element.8) | data formatting | bytes 2359296

commit v3 on v2

--- a/solution.py
+++ b/solution.py
@@ -23,10 +23,9 @@
 
 def kernel(
     xa_in, xg_in, valid_in, fa_in, fg_in, grad_in, bg_in, ba_in, sg_in, sa_in,
-    fa_out, fg_out, out_hbm,
-    fa_new, fg_new, out, out_sems,
+    fa_new, fg_new, out,
     xa, xg, valid, fa_old, fg_old, grad, bg, ba, sg, sa, in_sems, sa_col,
-    d_buf, r_buf, c_buf, b_buf, r_ba, az_s, az, cnt_y, cnt_s, cnt_z,
+    d_buf, r_buf, c_buf, b_buf, r_ba, acc, az_s, az, cnt_y, cnt_s, cnt_z,
     gz, rp_s, rp_r, pt, half_s, half_r, keep, rs_s, rs_r, sc,
     back, boy, pz_s, pz, py,
     gy_ss, gy_rs, g_ss, g_rs, f_ss, f_rs, rb1_ss, rb2_ss, rb3_ss, rb_rs,
@@ -256,6 +255,10 @@
         def _():
             far(y_lanes(rp_s, to), rp_r.at[k], gy_ss.at[k], gy_rs.at[k], y_dev(k)).start()
 
+    @each(NY, 0)
+    def _(k):
+        rows_x.along_x(k)
+
     rin = y_lanes(rp_s, y)[...].astype(F32)
     for k in range(1, NY):
         far(y_lanes(rp_s, y), rp_r.at[k], gy_ss.at[k], gy_rs.at[k], y_dev(k)).wait_recv()
@@ -295,10 +298,6 @@
     far(half_s.at[0], half_r.at[0], h_ss.at[0], h_rs.at[0], sib).wait_recv()
     keep[0] = keep[0] + half_r[0].astype(F32)
 
-    @each(NY, 0)
-    def _(k):
-        rows_x.along_x(k)
-
     @each(NQ)
     def _(k):
         far(rs_s.at[k], rs_r.at[k], p_ss.at[k], p_rs.at[k], q_dev(k)).wait_recv()
@@ -339,6 +338,8 @@
     def _(k):
         far(boy_own, boy_own, o_ss.at[k], o_rs.at[k], y_dev(k)).start()
 
+    rows_x.to_core()
+
     cols_step(2)
 
     @each(NY)
@@ -362,7 +363,6 @@
 
     each(NZ)(lambda k: pz_half(1, k).start())
 
-    rows_x.to_core()
     rows_x.arrive()
 
     @each(NY)
@@ -371,17 +371,18 @@
         far(tile, tile, n_ss.at[k], n_rs.at[k], y_dev(k)).wait_recv()
 
     cols_step(3)
+    for lo in (0, 256):
+        for i in range(NY):
+            rows = r_buf[i, :, :, lo : lo + 256].reshape(768, 256)
+            term = dot(rows, c_buf[i, :, lo : lo + 256], NT)
+            acc[:, lo : lo + 192] = term if i == 0 else acc[:, lo : lo + 192] + term
     cnt_s[...] = cnt_y[0] + cnt_y[1] + cnt_y[2] + cnt_y[3]
 
     @each(NZ, 0)
     def _(k):
         to = z_of(k)
-        ta = jnp.zeros((96, 192), F32)
-        tg = jnp.zeros((96, 192), F32)
-        for i in range(NY):
-            ta = ta + dot(r_buf[i, to, :, 0:256], c_buf[i, :, 0:256], NT)
-            tg = tg + dot(r_buf[i, to, :, 256:512], c_buf[i, :, 256:512], NT)
-        az_s[k] = jnp.concatenate([ta, tg], axis=1).astype(BF)
+        rows = pl.ds(pl.multiple_of(to * 96, 32), 96)
+        az_s[k] = jnp.concatenate([acc[rows, 0:192], acc[rows, 256:448]], axis=1).astype(BF)
 
         @pl.when(k > 0)
         def _():
@@ -401,20 +402,7 @@
         py[y, rows, :] = total.astype(BF)
         each(NY)(lambda k: py_half(h, k).start())
 
-    def store(i):
-        block = pl.ds(pl.multiple_of(z_of(i) * 384, 128), 384)
-        return pltpu.make_async_copy(out.at[:, block], out_hbm.at[:, block], out_sems.at[i])
-
-    fa_store = pltpu.make_async_copy(fa_new, fa_out, out_sems.at[8])
-    fg_store = pltpu.make_async_copy(fg_new, fg_out, out_sems.at[9])
-
-    def finish_factors(step):
-        if step > 0:
-            store(step).start()
-            store(NZ - step).start()
-            return
-        store(0).start()
-
+    def finish_factors():
         @each(NZ)
         def _(k):
             far(az_s.at[k], az.at[k], a_ss.at[k], a_rs.at[k], z_dev(k)).wait_recv()
@@ -428,8 +416,6 @@
         scale = (1.0 - DECAY) / count[0:1, 0:1]
         fa_new[...] = DECAY * fa_old[...] + stat[:, 0:192] * scale
         fg_new[...] = DECAY * fg_old[...] + stat[:, 192:384] * scale
-        fa_store.start()
-        fg_store.start()
 
     def ring_copy(h, way, k, arriving):
         at = z_of((NZ - 1, 1)[way] * (k + arriving))
@@ -451,14 +437,8 @@
                     ring_copy(h, way, k - 1, 1).wait_recv()
                 if k < 4:
                     ring_copy(h, way, k, 0).start()
-        if k < 4:
-            finish_factors(k)
-    store(4).start()
-
-    for i in range(NZ):
-        store(i).wait()
-    fa_store.wait()
-    fg_store.wait()
+        if k == 3:
+            finish_factors()
 
     @each(NY)
     def _(k):
@@ -511,7 +491,6 @@
     V = pltpu.VMEM
     dma = pltpu.SemaphoreType.DMA
     scratch = [
-        V((96, 192), F32), V((96, 192), F32), V((192, 3072), BF), dma((10,)),
         V((192, 256), BF), V((192, 256), BF), V((256,), jnp.int32),
         V((96, 192), F32), V((96, 192), F32), V((192, 96), BF),
         V((192, 3072), BF), V((192, 96), BF), V((3072,), F32), V((96,), F32), dma((10,)),
@@ -521,6 +500,7 @@
         V((4, 192, 512), BF),
         V((192, 128), BF),
         V((1024, 512), BF),
+        V((768, 512), F32),
         V((8, 96, 384), BF),
         V((8, 96, 384), BF),
         V((4, 8, 128), F32),
@@ -551,13 +531,9 @@
     ]
     return pl.pallas_call(
         kernel,
-        out_shape=(
-            jax.ShapeDtypeStruct((96, 192), F32),
-            jax.ShapeDtypeStruct((96, 192), F32),
-            jax.ShapeDtypeStruct((192, 3072), BF),
-        ),
+        out_shape=(V((96, 192), F32), V((96, 192), F32), V((192, 3072), BF)),
         in_specs=[pl.BlockSpec(memory_space=pltpu.HBM)] * 10,
-        out_specs=(pl.BlockSpec(memory_space=pltpu.HBM),) * 3,
+        out_specs=(pl.BlockSpec(memory_space=V),) * 3,
         scratch_shapes=scratch,
         compiler_params=pltpu.CompilerParams(
             collective_id=0, has_side_effects=True, vmem_limit_bytes=62 * 1024 * 1024

time: 118 us -> 113 us (0.958)
  local copies, waits for them, and re-layouts: 5.44 us -> 2.3 us
  Pallas kernels: 111 us -> 109 us
    unnamed x3, local copies, waits for them, and re-layouts: 5.44 us -> 2.3 us
    pallas_call x1, Pallas kernels: 111 us -> 109 us  [local(): pl.pallas_call(kernel, out_shape=(V((96, 192), F32), V((96, 192), F32), V...]
where the time goes in v3:
time: 113 us; the launch traced here: 112 us
  Pallas kernels  109 us (96%)
  local copies, waits for them, and re-layouts  2.3 us (2%)
    pallas_call x1, Pallas kernels, local(): pl.pallas_call(kernel, out_shape=(V((96, 192), F32), V((96, 192), F32), V...  109 us
    unnamed x3, local copies, waits for them, and re-layouts  2.3 us

profile of v3, /device:TPU:6, one launch (start us, length us, event | category | flops | bytes accessed | tf_op | source)
XLA Modules:
  0.0 112.2 jit_solution(17860305478089082061)
XLA Ops:
  0.6 109.2 %shard_map.121 = (f32[96,192]{1,0:T(8,128)S(1)}, f32[96,192]{1,0:T(8,128)S(1)}, bf16[192,3072]{1,0:T(8,128)(2,1)S(1)}) custom-call(bf16[192,256]{1,0:T(8,128)(2,1)} %bitcast.2, bf16[192,256]{1,0:T(8,128)(2,1)} %bitcast.3, s32[256]{0:T(256)} %valid_in.1, f32[96,192]{1,0:T(8,128)} %fa_in.1, f32[96,192]{1,0:T(8,128)} %fg_in.1, bf16[192,96]{1,0:T(8,128)(2,1)} %grad_in.1, ...), custom_call_target="tpu_custom_call" | custom-call | tf_op jit(solution)/shard_map/pallas_call | solution.py:532
  109.9 0.6 copy.16
  110.5 0.6 copy.17
  111.1 1.0 copy.18

commit v4 on v3

--- a/solution.py
+++ b/solution.py
@@ -28,8 +28,8 @@
     d_buf, r_buf, c_buf, b_buf, r_ba, acc, az_s, az, cnt_y, cnt_s, cnt_z,
     gz, rp_s, rp_r, pt, half_s, half_r, keep, rs_s, rs_r, sc,
     back, boy, pz_s, pz, py,
-    gy_ss, gy_rs, g_ss, g_rs, f_ss, f_rs, rb1_ss, rb2_ss, rb3_ss, rb_rs,
-    r1_ss, r2_ss, r3_ss, r_rs, c_ss, c_rs, n_ss, n_rs, m_ss, m_rs,
+    gy_ss, gy_rs, g_ss, g_rs, f_ss, f_rs, rb1_ss, rb2_ss, rb3_ss, rb1_rs, rb2_rs, rb3_rs,
+    r1_ss, r2_ss, r3_ss, r1_rs, r2_rs, r3_rs, c_ss, c_rs, n_ss, n_rs, m_ss, m_rs,
     h_ss, h_rs, p_ss, p_rs, s_ss, s_rs, sf_ss, sf_rs,
     a_ss, a_rs, o_ss, o_rs, z_ss, z_rs, q_ss, q_rs,
 ):
@@ -124,14 +124,16 @@
     pl.semaphore_wait(gate, 3 + 7 + 7 + 1 + 4 - jnp.where(own_piece, 1, 0))
 
     class Plane:
-        def __init__(self, src, slot, ss1, ss2, ss3, rs):
-            self.src, self.slot, self.ss1, self.ss2, self.ss3, self.rs = src, slot, ss1, ss2, ss3, rs
+        def __init__(self, src, slot, column, ss1, ss2, ss3, rs1, rs2, rs3):
+            self.src, self.slot, self.column = src, slot, column
+            self.ss1, self.ss2, self.ss3 = ss1, ss2, ss3
+            self.rs1, self.rs2, self.rs3 = rs1, rs2, rs3
 
         def piece(self, h, t):
             dev = (z * NY + 2 * c + h, (t * NX + x) * 2 + yh)
             itself = jnp.logical_and(dev[0] == r, dev[1] == s)
             src, dst = self.src.at[pl.ds(96 * h, 96), :], self.slot(y, q)
-            return itself, src, dst, far(src, dst, self.ss1.at[2 * h + t], self.rs.at[y, q], dev)
+            return itself, src, dst, far(src, dst, self.ss1.at[2 * h + t], self.rs1.at[y], dev)
 
         def along_y(self):
             for h in range(2):
@@ -144,38 +146,33 @@
 
                     @pl.when(itself)
                     def _():
-                        pltpu.make_async_copy(src, dst, self.rs.at[y, q]).start()
-
-        def along_x(self, k):
-            slot = self.slot(k, c * NX + x)
-            far(slot, slot, self.ss2.at[0, k], self.rs.at[k, c * NX + x], x_dev(1)).wait_recv()
-
-            @each(NX)
-            def _(j):
-                far(slot, slot, self.ss2.at[j, k], self.rs.at[k, c * NX + x], x_dev(j)).start()
-
-            far(slot, slot, self.ss3.at[0, k], self.rs.at[k, c * NX + x], sib).start()
+                        pltpu.make_async_copy(src, dst, self.rs1.at[y]).start()
+
+        def x_copy(self, j, back):
+            block = self.column(c * NX + lax.rem(x + NX - back, NX))
+            return far(block, block, self.ss2.at[j], self.rs2.at[j], x_dev(j))
+
+        def core_copy(self, j, core):
+            block = self.column(core * NX + lax.rem(x + NX - j, NX))
+            return far(block, block, self.ss3.at[j], self.rs3.at[j], sib)
+
+        def along_x(self):
+            @each(NY, 0)
+            def _(k):
+                slot = self.slot(k, c * NX + x)
+                far(slot, slot, self.ss1.at[0], self.rs1.at[k], sib).wait_recv()
+
+            each(NX)(lambda j: self.x_copy(j, 0).start())
+            self.core_copy(0, c).start()
 
         def to_core(self):
             @each(NX)
             def _(j):
-                col = c * NX + lax.rem(x + NX - j, NX)
-
-                @each(NY, 0)
-                def _(k):
-                    slot = self.slot(k, col)
-                    far(slot, slot, self.ss2.at[j, k], self.rs.at[k, col], x_dev(j)).wait_recv()
-                    far(slot, slot, self.ss3.at[j, k], self.rs.at[k, col], sib).start()
+                self.x_copy(j, j).wait_recv()
+                self.core_copy(j, c).start()
 
         def arrive(self):
-            @each(NX, 0)
-            def _(j):
-                col = (1 - c) * NX + j
-
-                @each(NY, 0)
-                def _(k):
-                    slot = self.slot(k, col)
-                    far(slot, slot, self.ss3.at[0, 0], self.rs.at[k, col], sib).wait_recv()
+            each(NX, 0)(lambda j: self.core_copy(j, 1 - c).wait_recv())
 
         def sent(self):
             for h in range(2):
@@ -186,40 +183,30 @@
                     def _():
                         copy.wait_send()
 
-            @each(NY, 0)
-            def _(k):
-                slot = self.slot(k, q)
-
-                @each(NX)
-                def _(j):
-                    far(slot, slot, self.ss2.at[j, k], self.rs.at[k, q], x_dev(j)).wait_send()
-
-                @each(NX, 0)
-                def _(j):
-                    far(slot, slot, self.ss3.at[j, k], self.rs.at[k, q], sib).wait_send()
+            each(NX)(lambda j: self.x_copy(j, 0).wait_send())
+            each(NX, 0)(lambda j: self.core_copy(j, c).wait_send())
 
     def ba_slot(k, col):
         return r_ba.at[pl.ds(pl.multiple_of(col * 128, 128), 96), pl.ds(pl.multiple_of(k * 128, 128), 128)]
 
-    rows_b = Plane(b_own, ba_slot, rb1_ss, rb2_ss, rb3_ss, rb_rs)
-    rows_x = Plane(d_buf, lambda k, col: r_buf.at[k, col], r1_ss, r2_ss, r3_ss, r_rs)
-
-    def during_first(k):
-        if k == 0:
-            rows_b.along_y()
-            c_own[:, 0:256] = (xa[...].astype(F32) * m).astype(BF)
-            c_own[:, 256:512] = (xg[...].astype(F32) * m).astype(BF)
-            cnt_y[y] = jnp.broadcast_to(jnp.sum(m, axis=1, keepdims=True), (8, 128))
-        else:
-            rows_b.along_x(k - 1)
+    def ba_column(col):
+        return r_ba.at[pl.ds(pl.multiple_of(col * 128, 128), 96), :]
+
+    rows_b = Plane(b_own, ba_slot, ba_column, rb1_ss, rb2_ss, rb3_ss, rb1_rs, rb2_rs, rb3_rs)
+    rows_x = Plane(
+        d_buf, lambda k, col: r_buf.at[col, k], lambda col: r_buf.at[col],
+        r1_ss, r2_ss, r3_ss, r1_rs, r2_rs, r3_rs,
+    )
 
     @each(NZ)
     def _(k):
         far(g_own, g_own, g_ss.at[k], g_rs.at[k], z_dev(k)).start()
 
-    for k in range(4):
-        during_first(k)
-    rows_b.along_x(3)
+    rows_b.along_y()
+    c_own[:, 0:256] = (xa[...].astype(F32) * m).astype(BF)
+    c_own[:, 256:512] = (xg[...].astype(F32) * m).astype(BF)
+    cnt_y[y] = jnp.broadcast_to(jnp.sum(m, axis=1, keepdims=True), (8, 128))
+    rows_b.along_x()
     rows_x.along_y()
     rows_b.to_core()
     rows_b.arrive()
@@ -255,9 +242,7 @@
         def _():
             far(y_lanes(rp_s, to), rp_r.at[k], gy_ss.at[k], gy_rs.at[k], y_dev(k)).start()
 
-    @each(NY, 0)
-    def _(k):
-        rows_x.along_x(k)
+    rows_x.along_x()
 
     rin = y_lanes(rp_s, y)[...].astype(F32)
     for k in range(1, NY):
@@ -373,7 +358,7 @@
     cols_step(3)
     for lo in (0, 256):
         for i in range(NY):
-            rows = r_buf[i, :, :, lo : lo + 256].reshape(768, 256)
+            rows = r_buf[:, i, :, lo : lo + 256].reshape(768, 256)
             term = dot(rows, c_buf[i, :, lo : lo + 256], NT)
             acc[:, lo : lo + 192] = term if i == 0 else acc[:, lo : lo + 192] + term
     cnt_s[...] = cnt_y[0] + cnt_y[1] + cnt_y[2] + cnt_y[3]
@@ -386,8 +371,25 @@
 
         @pl.when(k > 0)
         def _():
-            far(az_s.at[k], az.at[k], a_ss.at[k], a_rs.at[k], z_dev(k)).start()
             far(cnt_s, cnt_z.at[k], m_ss.at[k], m_rs.at[k], z_dev(k)).start()
+
+    def sum_rows(way, k):
+        return pl.ds(48 * way, 48) if k == 0 else pl.ds(0, 96)
+
+    def sum_copy(way, k):
+        rows = sum_rows(way, k)
+        return far(az_s.at[(4 - k, 4 + k)[way], rows, :], az.at[way, k, rows, :],
+                   a_ss.at[way, k], a_rs.at[way, k], z_dev((1, NZ - 1)[way]))
+
+    def sum_step(k):
+        for way in range(2):
+            if k > 0:
+                sum_copy(way, k - 1).wait_recv()
+                rows, at = sum_rows(way, k - 1), (4 - k, 4 + k)[way]
+                az_s[at, rows, :] = (az_s[at, rows, :].astype(F32) + az[way, k - 1, rows, :].astype(F32)).astype(BF)
+            sum_copy(way, k).start()
+
+    sum_step(0)
 
     def py_half(h, k):
         slot = py.at[y, pl.ds(96 * h, 96), :]
@@ -405,17 +407,19 @@
     def finish_factors():
         @each(NZ)
         def _(k):
-            far(az_s.at[k], az.at[k], a_ss.at[k], a_rs.at[k], z_dev(k)).wait_recv()
             far(cnt_s, cnt_z.at[k], m_ss.at[k], m_rs.at[k], z_dev(k)).wait_recv()
 
-        stat = az_s[0].astype(F32)
+        for way in range(2):
+            sum_copy(way, 3).wait_recv()
+        stat = az_s[0].astype(F32) + az[0, 3].astype(F32) + az[1, 3].astype(F32)
         count = cnt_s[...]
         for k in range(1, NZ):
-            stat = stat + az[k].astype(F32)
             count = count + cnt_z[k]
         scale = (1.0 - DECAY) / count[0:1, 0:1]
         fa_new[...] = DECAY * fa_old[...] + stat[:, 0:192] * scale
         fg_new[...] = DECAY * fg_old[...] + stat[:, 192:384] * scale
+
+    sum_step(1)
 
     def ring_copy(h, way, k, arriving):
         at = z_of((NZ - 1, 1)[way] * (k + arriving))
@@ -437,6 +441,10 @@
                     ring_copy(h, way, k - 1, 1).wait_recv()
                 if k < 4:
                     ring_copy(h, way, k, 0).start()
+        if k == 0:
+            sum_step(2)
+        if k == 1:
+            sum_step(3)
         if k == 3:
             finish_factors()
 
@@ -453,7 +461,6 @@
         far(rs_s.at[k], rs_r.at[k], p_ss.at[k], p_rs.at[k], q_dev(k)).wait_send()
         far(sc_own, sc_own, s_ss.at[k], s_rs.at[k], q_dev(k)).wait_send()
         far(g_own, g_own, g_ss.at[k], g_rs.at[k], z_dev(k)).wait_send()
-        far(az_s.at[k], az.at[k], a_ss.at[k], a_rs.at[k], z_dev(k)).wait_send()
         far(cnt_s, cnt_z.at[k], m_ss.at[k], m_rs.at[k], z_dev(k)).wait_send()
         pz_half(0, k).wait_send()
         pz_half(1, k).wait_send()
@@ -466,6 +473,10 @@
     for d in range(NY - 1):
         for ok, onward, copy in cols_copies(d):
             pl.when(onward)(copy.wait_send)
+
+    for k in range(4):
+        for way in range(2):
+            sum_copy(way, k).wait_send()
 
     rows_b.sent()
     rows_x.sent()
@@ -496,13 +507,13 @@
         V((192, 3072), BF), V((192, 96), BF), V((3072,), F32), V((96,), F32), dma((10,)),
         V((96, 1), F32),
         V((192, 512), BF),
-        V((4, 8, 96, 512), BF),
+        V((8, 4, 96, 512), BF),
         V((4, 192, 512), BF),
         V((192, 128), BF),
         V((1024, 512), BF),
         V((768, 512), F32),
         V((8, 96, 384), BF),
-        V((8, 96, 384), BF),
+        V((2, 4, 96, 384), BF),
         V((4, 8, 128), F32),
         V((8, 128), F32),
         V((8, 8, 128), F32),
@@ -523,11 +534,11 @@
         V((4, 192, 128), BF),
         dma((4,)), dma((4,)),
         dma((8,)), dma((8,)), dma((2, 2, 4)), dma((2, 2, 4)),
-        dma((4,)), dma((4, 4)), dma((4, 4)), dma((4, 8)),
-        dma((4,)), dma((4, 4)), dma((4, 4)), dma((4, 8)),
+        *[dma((4,))] * 6,
+        *[dma((4,))] * 6,
         dma((2, 4)), dma((4,)), dma((4,)), dma((4,)), dma((8,)), dma((8,)),
         dma((8,)), dma((8,)), dma((8,)), dma((8,)), dma((8,)), dma((8,)), dma((8,)), dma((8,)),
-        dma((8,)), dma((8,)), dma((4,)), dma((4,)), dma((2, 8)), dma((2, 8)), dma((2, 4)), dma((2, 4)),
+        dma((2, 4)), dma((2, 4)), dma((4,)), dma((4,)), dma((2, 8)), dma((2, 8)), dma((2, 4)), dma((2, 4)),
     ]
     return pl.pallas_call(
         kernel,

time: 113 us -> 108 us (0.956)
  Pallas kernels: 109 us -> 105 us
    pallas_call x1, Pallas kernels: 109 us -> 105 us  [local(): pl.pallas_call(kernel, out_shape=(V((96, 192), F32), V((96, 192), F32), V...]
where the time goes in v4:
time: 108 us
  Pallas kernels  105 us (97%)
  local copies, waits for them, and re-layouts  2.3 us (2%)
    pallas_call x1, Pallas kernels, local(): pl.pallas_call(kernel, out_shape=(V((96, 192), F32), V((96, 192), F32), V...  105 us
    unnamed x3, local copies, waits for them, and re-layouts  2.3 us

profile of v4, /device:TPU:6, one launch (start us, length us, event | category | flops | bytes accessed | tf_op | source)
XLA Modules:
  0.0 107.8 jit_solution(5256771350568974600)
XLA Ops:
  0.6 104.8 %shard_map.121 = (f32[96,192]{1,0:T(8,128)S(1)}, f32[96,192]{1,0:T(8,128)S(1)}, bf16[192,3072]{1,0:T(8,128)(2,1)S(1)}) custom-call(bf16[192,256]{1,0:T(8,128)(2,1)} %bitcast.2, bf16[192,256]{1,0:T(8,128)(2,1)} %bitcast.3, s32[256]{0:T(256)} %valid_in.1, f32[96,192]{1,0:T(8,128)} %fa_in.1, f32[96,192]{1,0:T(8,128)} %fg_in.1, bf16[192,96]{1,0:T(8,128)(2,1)} %grad_in.1, ...), custom_call_target="tpu_custom_call" | custom-call | tf_op jit(solution)/shard_map/pallas_call | solution.py:543
  105.5 0.6 copy.16
  106.1 0.6 copy.17
  106.8 1.0 copy.18

commit v5 on v4

--- a/solution.py
+++ b/solution.py
@@ -47,7 +47,10 @@
         return lax.rem(z + k, NZ)
 
     def q_of(k):
-        return lax.rem(q + k, NQ)
+        return lax.rem(yh + k // NX, 2) * NX + lax.rem(x + k % NX, NX)
+
+    def q_from(k):
+        return lax.rem(yh + k // NX, 2) * NX + lax.rem(x + NX - k % NX, NX)
 
     def y_dev(k):
         return (z * NY + y_of(k), s)
@@ -198,8 +201,12 @@
         r1_ss, r2_ss, r3_ss, r1_rs, r2_rs, r3_rs,
     )
 
+    def opposite_first(j):
+        return (j + 2) % 7 + 1
+
     @each(NZ)
-    def _(k):
+    def _(j):
+        k = opposite_first(j)
         far(g_own, g_own, g_ss.at[k], g_rs.at[k], z_dev(k)).start()
 
     rows_b.along_y()
@@ -255,21 +262,23 @@
     sa_row = jnp.concatenate([sa[...].reshape(1, 96), jnp.zeros((1, 32), F32)], axis=1)
     sa_col[...] = jnp.broadcast_to(sa_row, (128, 128)).T[0:96, 0:1]
 
-    def e_block(ref, k, rows=slice(None)):
-        return ref.at[rows, pl.ds(pl.multiple_of(q_of(k) * 384, 128), 384)]
+    def e_block(ref, chip, rows=slice(None)):
+        return ref.at[rows, pl.ds(pl.multiple_of(chip * 384, 128), 384)]
 
     mine = pl.ds(pl.multiple_of(c * 48, 16), 48)
     other = pl.ds(pl.multiple_of((1 - c) * 48, 16), 48)
 
     @each(NQ, 0)
-    def _(k):
-        pt[...] = dot(rin, e_block(bg, k)[...])
+    def _(j):
+        k = NQ - 1 - j
+        pt[...] = dot(rin, e_block(bg, q_of(k))[...])
         keep[k] = pt[mine, :]
         half_s[k] = pt[other, :].astype(BF)
         far(half_s.at[k], half_r.at[k], h_ss.at[k], h_rs.at[k], sib).start()
 
     @each(NQ)
-    def _(k):
+    def _(j):
+        k = NQ - j
         far(half_s.at[k], half_r.at[k], h_ss.at[k], h_rs.at[k], sib).wait_recv()
         rs_s[k] = (keep[k] + half_r[k].astype(F32)).astype(BF)
         far(rs_s.at[k], rs_r.at[k], p_ss.at[k], p_rs.at[k], q_dev(k)).start()
@@ -290,20 +299,22 @@
 
     sg_here = sg[pl.ds(pl.multiple_of(q * 384, 128), 384)].reshape(1, 384)
     denominator = sa_col[mine, :] * sg_here + DAMPING
-    sc_own = e_block(sc, 0, mine)
+    sc_own = e_block(sc, q, mine)
     sc_own[...] = (keep[0] / denominator).astype(BF)
 
     @each(NQ)
-    def _(k):
+    def _(j):
+        k = NQ - j
         far(sc_own, sc_own, s_ss.at[k], s_rs.at[k], q_dev(k)).start()
 
     far(sc_own, sc_own, sf_ss.at[0], sf_rs.at[0], sib).start()
 
     cols_step(1)
+    rows_x.to_core()
 
     @each(NQ)
     def _(k):
-        got = e_block(sc, NQ - k, mine)
+        got = e_block(sc, q_from(k), mine)
         far(got, got, s_ss.at[k], s_rs.at[k], q_dev(k)).wait_recv()
         far(got, got, sf_ss.at[k], sf_rs.at[k], sib).start()
 
@@ -311,9 +322,9 @@
 
     @each(NQ, 0)
     def _(k):
-        got = e_block(sc, NQ - k, other)
+        got = e_block(sc, q_from(k), other)
         far(got, got, sf_ss.at[k], sf_rs.at[k], sib).wait_recv()
-        back[...] += dot(e_block(bg, NQ - k)[...], e_block(sc, NQ - k)[...], NT)
+        back[...] += dot(e_block(bg, q_from(k))[...], e_block(sc, q_from(k))[...], NT)
 
     boy_own = y_lanes(boy, y)
     boy_own[:, 0:96] = back[...].astype(BF)
@@ -323,8 +334,6 @@
     def _(k):
         far(boy_own, boy_own, o_ss.at[k], o_rs.at[k], y_dev(k)).start()
 
-    rows_x.to_core()
-
     cols_step(2)
 
     @each(NY)
@@ -337,7 +346,8 @@
         return far(pz_s.at[k, rows, :], pz.at[k, rows, :], z_ss.at[h, k], z_rs.at[h, k], z_dev(k))
 
     @each(NZ + 1)
-    def _(k):
+    def _(j):
+        k = jnp.where(j < NZ, opposite_first(j), NZ)
         to = z_of(k)
         rows = r_ba[pl.ds(pl.multiple_of(to * 128, 128), 128), :]
         pz_s[k] = dot(boy[...], rows, NT).astype(BF)
@@ -346,7 +356,7 @@
         def _():
             pz_half(0, k).start()
 
-    each(NZ)(lambda k: pz_half(1, k).start())
+    each(NZ)(lambda j: pz_half(1, opposite_first(j)).start())
 
     rows_x.arrive()
 

time: 108 us -> 108 us (level)
  no operation moved by 1% of the time
where the time goes in v5:
time: 108 us; the launch traced here: 107 us
  Pallas kernels  105 us (97%)
  local copies, waits for them, and re-layouts  2.3 us (2%)
    pallas_call x1, Pallas kernels, local(): pl.pallas_call(kernel, out_shape=(V((96, 192), F32), V((96, 192), F32), V...  105 us
    unnamed x3, local copies, waits for them, and re-layouts  2.3 us

profile of v5, /device:TPU:6, one launch (start us, length us, event | category | flops | bytes accessed | tf_op | source)
XLA Modules:
  0.0 107.5 jit_solution(4013807845867786391)
XLA Ops:
  0.6 104.5 %shard_map.121 = (f32[96,192]{1,0:T(8,128)S(1)}, f32[96,192]{1,0:T(8,128)S(1)}, bf16[192,3072]{1,0:T(8,128)(2,1)S(1)}) custom-call(bf16[192,256]{1,0:T(8,128)(2,1)} %bitcast.2, bf16[192,256]{1,0:T(8,128)(2,1)} %bitcast.3, s32[256]{0:T(256)} %valid_in.1, f32[96,192]{1,0:T(8,128)} %fa_in.1, f32[96,192]{1,0:T(8,128)} %fg_in.1, bf16[192,96]{1,0:T(8,128)(2,1)} %grad_in.1, ...), custom_call_target="tpu_custom_call" | custom-call | tf_op jit(solution)/shard_map/pallas_call | solution.py:553
  105.2 0.6 copy.16
  105.8 0.6 copy.17
  106.5 1.0 copy.18
